TPU v7x, 256 devices: a whole 4x4x8 slice. The times are simulated.
256 devices in a mesh: seq: 64 (over y, z, core), head: 4 (over x).
Axes of the slice: x: 4, y: 4, z: 8, core: 2. Of those that a mesh axis runs over, the one named last changes fastest.
Arguments:
- queries: bfloat16 [8192, 64, 128], P('seq', 'head'), may hold values from -6 to 6
- keys: bfloat16 [8192, 64, 128], P('seq', 'head'), may hold values from -6 to 6
- values: bfloat16 [8192, 64, 128], P('seq', 'head'), may hold values from -15 to 15
- out_grad: bfloat16 [8192, 64, 128], P('seq', 'head'), may hold values from -6 to 6
Outputs:
- normed: bfloat16 [8192, 64, 128], P('seq', 'head')
- query_grad: bfloat16 [8192, 64, 128], P('seq', 'head')
- key_grad: bfloat16 [8192, 64, 128], P('seq', 'head')
- value_grad: bfloat16 [8192, 64, 128], P('seq', 'head')
All inputs are finite; a program needn't handle non-finite values.
Results may differ from a plain program's by a relative error of at most 0.0058.
Values sent between devices are 32-bit elements; how exact they have to be, the bound alone decides.
A program may use at most 256 MiB of HBM per device.

v0:
```python
import jax
import jax.numpy as jnp
from jax import lax
from jax.sharding import PartitionSpec as P

EPS = 1e-06


def prefix(value, axis, join, neutral, backward):
    count, mine = (lax.axis_size(axis), lax.axis_index(axis))
    pieces = lax.all_gather(value, axis)
    if backward:
        pieces = pieces[::-1]
        mine = count - 1 - mine
    running = jnp.full_like(value, 0) + jnp.asarray(neutral, value.dtype)

    def step(position, running):
        longer = join(running, pieces[position])
        return jnp.where(position < mine, longer, running)

    return lax.fori_loop(0, count - 1, step, running)


def add_states(earlier, latter):
    return earlier + latter


def batched(left, right, left_contract, right_contract):
    return lax.dot_general(
        left,
        right,
        (((left_contract,), (right_contract,)), ((0,), (0,))),
        preferred_element_type=jnp.float32,
    )


def shards(queries, keys, values, out_grad):
    tok_rows, head_count, head_dim = queries.shape
    row_width = lax.axis_size("head") * head_count * head_dim
    causal = jnp.tril(jnp.ones((tok_rows, tok_rows), dtype=bool))[None, :, :]
    f32 = jnp.float32
    query_hm = jnp.swapaxes(queries, 0, 1)
    key_hm = jnp.swapaxes(keys, 0, 1)
    value_hm = jnp.swapaxes(values, 0, 1)
    grad_hm = jnp.swapaxes(out_grad, 0, 1).astype(f32)
    scores = batched(query_hm, key_hm, 2, 2)
    weights = jnp.where(causal, scores, 0.0).astype(jnp.bfloat16)
    own_state = batched(key_hm, value_hm, 1, 1)
    zero_state = jnp.zeros_like(own_state)
    earlier_sum = prefix(own_state, "seq", add_states, zero_state, False)
    prior = earlier_sum.astype(jnp.bfloat16)
    attended = batched(weights, value_hm, 2, 1) + batched(query_hm, prior, 2, 1)
    square_sum, dot_sum = lax.psum(
        (jnp.sum(attended * attended, axis=(0, 2)), jnp.sum(grad_hm * attended, axis=(0, 2))),
        "head",
    )
    inv_rms = 1.0 / jnp.sqrt(square_sum / row_width + EPS)
    normed = (attended * inv_rms[None, :, None]).astype(jnp.bfloat16)
    factor = inv_rms * inv_rms * inv_rms * dot_sum / row_width
    att_grad = (inv_rms[None, :, None] * grad_hm - attended * factor[None, :, None]).astype(
        jnp.bfloat16
    )
    grad_scores = batched(att_grad, value_hm, 2, 2)
    masked = jnp.where(causal, grad_scores, 0.0).astype(jnp.bfloat16)
    own_grad = batched(query_hm, att_grad, 1, 1)
    later_sum = prefix(own_grad, "seq", add_states, zero_state, True)
    later = later_sum.astype(jnp.bfloat16)
    query_grad = batched(masked, key_hm, 2, 1) + batched(att_grad, prior, 2, 2)
    key_grad = batched(masked, query_hm, 1, 1) + batched(value_hm, later, 2, 2)
    value_grad = batched(weights, att_grad, 1, 1) + batched(key_hm, later, 2, 1)
    return (
        jnp.swapaxes(normed, 0, 1),
        jnp.swapaxes(query_grad.astype(jnp.bfloat16), 0, 1),
        jnp.swapaxes(key_grad.astype(jnp.bfloat16), 0, 1),
        jnp.swapaxes(value_grad.astype(jnp.bfloat16), 0, 1),
    )


def solution(mesh):
    return jax.shard_map(
        shards,
        mesh=mesh,
        in_specs=(
            P("seq", "head", None),
            P("seq", "head", None),
            P("seq", "head", None),
            P("seq", "head", None),
        ),
        out_specs=(
            P("seq", "head", None),
            P("seq", "head", None),
            P("seq", "head", None),
            P("seq", "head", None),
        ),
        check_vma=False,
    )
```

profile of v0, /device:TPU:1, one launch (start us, length us, event | category | flops | bytes accessed | tf_op | source)
XLA Modules:
  0.0 763.6 jit_solution(2822661834630201227)
XLA Ops:
  8.2 2.4 fusion.17
  12.2 2.7 fusion.2
  14.8 236.6 %all-gather.5.cloned.1.call-done = f32[1024,128,128]{2,1,0:T(8,128)} async-done(((f32[16,128,128]{2,1,0:T(8,128)}), f32[1024,128,128]{2,1,0:T(8,128)}) %all-gather.5.cloned.1.call-update) | async-done | bytes 67108880 | tf_op jit(solution)/shard_map/all_gather | solution.py:11
  251.4 101.6 %while.28 = (s32[]{:T(128)}, f32[16,128,128]{2,1,0:T(8,128)S(1)}, s32[]{:T(128)}, f32[64,16,128,128]{3,2,1,0:T(8,128)}, s32[]{:T(128)}, /*index=5*/s32[]{:T(128)}) while((s32[]{:T(128)}, f32[16,128,128]{2,1,0:T(8,128)S(1)}, s32[]{:T(128)}, f32[64,16,128,128]{3,2,1,0:T(8,128)}, s32[]{:T(128)}, /*index=5*/s32[]{:T(128)}) %tuple.68), condition=%wide.region_1.2_spmd.clone, body=%wide.region_0.1_spmd.clone.sunk | while | flops 786436 | bytes 3145829 | solution.py:21
  253.0 1.6 add_select_fusion.4
  254.6 1.6 add_select_fusion.4
  256.2 1.6 add_select_fusion.4
  261.1 1.6 add_select_fusion.4
  262.7 1.6 add_select_fusion.4
  264.3 1.6 add_select_fusion.4
  267.5 1.6 add_select_fusion.4
  269.1 1.6 add_select_fusion.4
  270.7 1.6 add_select_fusion.4
  272.4 1.6 add_select_fusion.4
  275.6 1.6 add_select_fusion.4
  277.2 1.6 add_select_fusion.4
  278.8 1.6 add_select_fusion.4
  283.7 1.6 add_select_fusion.4
  285.3 1.6 add_select_fusion.4
  286.9 1.6 add_select_fusion.4
  291.7 1.6 add_select_fusion.4
  293.3 1.6 add_select_fusion.4
  294.9 1.6 add_select_fusion.4
  298.2 1.6 add_select_fusion.4
  299.8 1.6 add_select_fusion.4
  301.4 1.6 add_select_fusion.4
  303.0 1.6 add_select_fusion.4
  306.2 1.6 add_select_fusion.4
  307.9 1.6 add_select_fusion.4
  309.5 1.6 add_select_fusion.4
  314.3 1.6 add_select_fusion.4
  315.9 1.6 add_select_fusion.4
  317.5 1.6 add_select_fusion.4
  322.4 1.6 add_select_fusion.4
  324.0 1.6 add_select_fusion.4
  325.6 1.6 add_select_fusion.4
  328.8 1.6 add_select_fusion.4
  330.5 1.6 add_select_fusion.4
  332.1 1.6 add_select_fusion.4
  333.7 1.6 add_select_fusion.4
  336.9 1.6 add_select_fusion.4
  338.5 1.6 add_select_fusion.4
  340.1 1.6 add_select_fusion.4
  345.0 1.6 add_select_fusion.4
  346.6 1.6 add_select_fusion.4
  348.2 1.6 add_select_fusion.4
  354.6 2.9 fusion.10
  357.5 8.4 %all-reduce = (f32[128]{0:T(128)S(1)}, f32[128]{0:T(128)S(1)}) all-reduce(f32[128]{0:T(128)S(1)} %get-tuple-element.203, f32[128]{0:T(128)S(1)} %get-tuple-element.202), channel_id=1, replica_groups=mesh['seq'=64,'head'=4] {'head'}, use_global_device_ids=true, to_apply=%region_3.4 | all-reduce | flops 256 | bytes 2048 | tf_op jit(solution)/shard_map/psum | solution.py:53
  365.8 1.6 fusion.9
  367.5 2.3 convolution_bitcast_fusion.3
  369.8 2.5 copy.50
  372.4 2.5 fusion.12
  374.8 2.2 copy.58
  380.6 2.6 convolution_bitcast_fusion.1
  383.2 2.5 convolution_bitcast_fusion.4
  385.7 220.0 %all-gather.7.cloned.1.call-done = f32[1024,128,128]{2,1,0:T(8,128)} async-done(((f32[16,128,128]{2,1,0:T(8,128)}), f32[1024,128,128]{2,1,0:T(8,128)}) %all-gather.7.cloned.1.call-update) | async-done | bytes 67108880 | tf_op jit(solution)/shard_map/all_gather | solution.py:11
  605.7 43.9 %rev.3 = f32[64,16,128,128]{3,2,1,0:T(8,128)} reverse(f32[64,16,128,128]{3,2,1,0:T(8,128)} %bitcast.11), dimensions={0} | reverse | bytes 134217728 | tf_op jit(solution)/shard_map/rev | solution.py:13
  649.6 101.7 %while.29 = (s32[]{:T(128)}, f32[16,128,128]{2,1,0:T(8,128)S(1)}, s32[]{:T(128)}, f32[64,16,128,128]{3,2,1,0:T(8,128)}, s32[]{:T(128)}, /*index=5*/s32[]{:T(128)}) while((s32[]{:T(128)}, f32[16,128,128]{2,1,0:T(8,128)S(1)}, s32[]{:T(128)}, f32[64,16,128,128]{3,2,1,0:T(8,128)}, s32[]{:T(128)}, /*index=5*/s32[]{:T(128)}) %tuple.71), condition=%wide.region_7.8_spmd.clone, body=%wide.region_6.7_spmd.clone.sunk | while | flops 786436 | bytes 3145829 | solution.py:21
  651.2 1.6 add_select_fusion.5
  654.4 1.6 add_select_fusion.5
  657.7 1.6 add_select_fusion.5
  660.9 1.6 add_select_fusion.5
  664.1 1.6 add_select_fusion.5
  751.3 1.7 fusion.5
  (104 shorter events, 137.0 us)
Async XLA Ops:
  7.2 1.0 copy-start
  7.2 244.2 %all-gather.5.cloned.1.call-start = ((), (), s32[]{:S(2)}) async-start(), calls=%async_computation | async-start | bytes 68157440 | tf_op jit(solution)/shard_map/all_gather | solution.py:11
  10.6 595.1 %all-gather.7.cloned.1.call-start = ((), (), s32[]{:S(2)}) async-start(), calls=%async_computation.1 | async-start | bytes 68157440 | tf_op jit(solution)/shard_map/all_gather | solution.py:11
  12.1 353.7 %copy-start.2 = (bf16[128,16,128]{0,2,1:T(8,128)(2,1)}, bf16[128,16,128]{0,2,1:T(8,128)(2,1)S(1)}, u32[]{:S(2)}) copy-start(bf16[128,16,128]{0,2,1:T(8,128)(2,1)S(1)} %copy.42) | copy-start | bytes 1572868
  354.6 17.8 %copy-start.1 = (f32[16,128,128]{2,1,0:T(8,128)}, f32[16,128,128]{2,1,0:T(8,128)S(1)}, u32[]{:S(2)}) copy-start(f32[16,128,128]{2,1,0:T(8,128)S(1)} %fusion.26) | copy-start | bytes 3145732
  605.7 147.3 %copy-start.3 = (bf16[128,16,128]{2,1,0:T(8,128)(2,1)S(1)}, bf16[128,16,128]{2,1,0:T(8,128)(2,1)}, u32[]{:S(2)}) copy-start(bf16[128,16,128]{2,1,0:T(8,128)(2,1)} %param.9) | copy-start | bytes 1572868
Sparse Core Ops, SparseCore 0:
  10.8 240.5 all-gather.4
  372.5 233.1 all-gather.6
where the time goes:
time: 769 us; the launch traced here: 764 us
  waiting for transfers between devices  457 us (59%)
  other arithmetic  204 us (27%)
  local copies, waits for them, and re-layouts  54.5 us (7%)
  matrix products  22.5 us (3%)
  between operations  14.2 us (2%)
  blocking collectives  8.37 us (1%)
    all_gather x2, waiting for transfers between devices, prefix(): pieces = lax.all_gather(value, axis)  457 us
    select_n x126, other arithmetic, step(): return jnp.where(position < mine, longer, running)  200 us
    rev x1, local copies, waits for them, and re-layouts, prefix(): pieces = pieces[::-1]  43.9 us
    dot_general x12, matrix products, batched(): lax.dot_general(left, right, (((left_contract,), (right_contract,)), ((0,...  22.5 us
  transfers between devices with their start and end apart: 2, of which 2 were waited for; matrix products, arithmetic and copies ran while one was open for 2% of the time, Pallas kernels for 0%

commit v1 on v0

v1 whole, which is shorter than its diff:
```python
import jax
import jax.numpy as jnp
from jax import lax
from jax.experimental import pallas as pl
from jax.experimental.pallas import tpu as pltpu
from jax.sharding import PartitionSpec as P

EPS = 1e-06
CHIPS = 32
TOK = 128
NH = 16
DH = 128
HALF = NH // 2
ROWS = HALF * DH // CHIPS
SPLIT = DH // ROWS
ROW_WIDTH = 64 * DH
MESH = pl.DeviceIdType.MESH
F32 = jnp.float32
BF16 = jnp.bfloat16


def mm(left, right, lc, rc):
    return lax.dot_general(
        left, right, (((lc,), (rc,)), ((), ())), preferred_element_type=F32
    )


def kernel(
    q_hbm, k_hbm, v_hbm, g_hbm,
    n_out, qg_out, kg_out, vg_out,
    q_in, k_in, v_in, g_in, n_vm, qg_vm, kg_vm, vg_vm,
    flat_a, flat_b, qh, kh, vh, gh, wts, att, agr, prior, kg_acc, vg_acc,
    state, sib, chip, owned, bases, base, share, other,
    acc, msg, sums,
    load_sem, store_sem, d2d_send, d2d_recv, a2a_send, a2a_recv, x_send, x_recv,
):
    seq, head = lax.axis_index("seq"), lax.axis_index("head")
    s, c = seq // 2, lax.rem(seq, 2)
    oc = 1 - c

    bar = pltpu.get_barrier_semaphore()

    def greet(i, _):
        t = lax.rem(s + i, CHIPS)
        pl.semaphore_signal(bar, inc=1, device_id=(2 * t + c, head), device_id_type=MESH)
        return 0

    pl.semaphore_signal(bar, inc=1, device_id=(2 * s + oc, head), device_id_type=MESH)
    for i in range(1, 4):
        pl.semaphore_signal(
            bar, inc=1, device_id=(seq, lax.rem(head + i, 4)), device_id_type=MESH
        )
    lax.fori_loop(1, CHIPS, greet, 0)

    loads = [
        pltpu.make_async_copy(src, dst, load_sem.at[i])
        for i, (src, dst) in enumerate(
            ((k_hbm, k_in), (v_hbm, v_in), (q_hbm, q_in), (g_hbm, g_in))
        )
    ]
    for ld in loads:
        ld.start()

    def flatten(src, flat):
        flat[...] = src[...].astype(F32).reshape(TOK * NH, DH)

    def pick(flat, h):
        return flat[pl.ds(h, TOK, stride=NH), :].astype(BF16)

    def over(count, body):
        def step(i, _):
            for u in range(4):
                body(4 * i + u)
            return 0

        lax.fori_loop(0, count // 4, step, 0)

    rows = lax.broadcasted_iota(jnp.int32, (TOK, TOK), 0)
    cols = lax.broadcasted_iota(jnp.int32, (TOK, TOK), 1)
    causal = cols <= rows

    def d2d(k, src, dst):
        return pltpu.make_async_remote_copy(
            src_ref=src, dst_ref=dst, send_sem=d2d_send.at[k], recv_sem=d2d_recv.at[k],
            device_id=(2 * s + oc, head), device_id_type=MESH,
        )

    def spread(k, src, dst):
        def send(i, _):
            t = lax.rem(s + i, CHIPS)
            pltpu.make_async_remote_copy(
                src_ref=src.at[t], dst_ref=dst.at[s], send_sem=a2a_send.at[k],
                recv_sem=a2a_recv.at[k], device_id=(2 * t + c, head), device_id_type=MESH,
            ).start()
            return 0

        lax.fori_loop(1, CHIPS, send, 0)
        dst[s] = src[s]

    def spread_wait(k, src, dst):
        return pltpu.make_async_remote_copy(
            src_ref=src.at[pl.ds(0, CHIPS - 1)], dst_ref=dst.at[pl.ds(0, CHIPS - 1)],
            send_sem=a2a_send.at[k], recv_sem=a2a_recv.at[k],
            device_id=(2 * s + oc, head), device_id_type=MESH,
        )

    def put_state(j, h, value):
        state[j, pl.ds(h * SPLIT, SPLIT)] = value.reshape(SPLIT, ROWS, DH)

    def scan(j, make_other, make_own, during_up, during_down, reverse):
        make_other()
        if j == 0:
            pl.semaphore_wait(bar, CHIPS - 1 + 4)
        out = d2d(2 * j, state.at[j, pl.ds(oc * CHIPS, CHIPS)], sib.at[j])
        out.start()
        make_own()
        out.wait_recv()
        chip[j] = state[j, pl.ds(c * CHIPS, CHIPS)] + sib[j]
        spread(2 * j, chip.at[j], owned.at[j])
        during_up()
        spread_wait(2 * j, chip.at[j], owned.at[j]).wait_recv()
        run = jnp.zeros((ROWS, DH), F32)
        for t in range(CHIPS - 1, -1, -1) if reverse else range(CHIPS):
            bases[j, t] = run
            run = run + owned[j, t]
        spread(2 * j + 1, bases.at[j], base.at[j])
        during_down()
        spread_wait(2 * j + 1, bases.at[j], base.at[j]).wait_recv()
        first = oc if reverse else c
        share[j] = base[j] + jnp.where(first == 0, state[j, pl.ds(c * CHIPS, CHIPS)], 0.0)
        back = d2d(2 * j + 1, share.at[j], other.at[j])
        back.start()
        base[j] = base[j] + jnp.where(first == 1, sib[j], 0.0)
        return out, back

    def scan_end(j, out, back):
        out.wait_send()
        back.wait_send()
        spread_wait(2 * j, chip.at[j], owned.at[j]).wait_send()
        spread_wait(2 * j + 1, bases.at[j], base.at[j]).wait_send()

    def head_of(ref, j, i):
        return ref[j, pl.ds(i * SPLIT, SPLIT)].reshape(DH, DH).astype(BF16)

    loads[0].wait()
    flatten(k_in, flat_a)
    loads[1].wait()
    flatten(v_in, flat_b)

    def make_state(h):
        kk, vv = pick(flat_a, h), pick(flat_b, h)
        kh[h], vh[h] = kk, vv
        put_state(0, h, mm(kk, vv, 0, 0))

    def local_attention():
        loads[2].wait()
        flatten(q_in, flat_a)

        def body(h):
            qq = pick(flat_a, h)
            qh[h] = qq
            w = jnp.where(causal, mm(qq, kh[h], 1, 1), 0.0).astype(BF16)
            wts[h] = w
            att[h] = mm(w, vh[h], 1, 0)

        over(NH, body)

    def load_grads():
        loads[3].wait()
        flatten(g_in, flat_b)

        def body(h):
            gh[h] = pick(flat_b, h)

        over(NH, body)
        acc[...] = jnp.zeros_like(acc)

    out0, back0 = scan(
        0,
        lambda: over(HALF, lambda i: make_state(oc * HALF + i)),
        lambda: over(HALF, lambda i: make_state(c * HALF + i)),
        local_attention,
        load_grads,
        False,
    )

    def attend(h, pr):
        prior[h] = pr
        a = att[h] + mm(qh[h], pr, 1, 0)
        att[h] = a
        acc[0] += a * a
        acc[1] += a * gh[h].astype(F32)

    over(HALF, lambda i: attend(c * HALF + i, head_of(base, 0, i)))
    back0.wait_recv()
    over(HALF, lambda i: attend(oc * HALF + i, head_of(other, 0, i)))

    sq = jnp.sum(acc[0], axis=1, keepdims=True)
    dt = jnp.sum(acc[1], axis=1, keepdims=True)
    packed = jnp.where(cols == 0, sq, jnp.where(cols == 1, dt, 0.0))
    msg[...] = jnp.transpose(packed)[0:8]
    xs = [
        pltpu.make_async_remote_copy(
            src_ref=msg, dst_ref=sums.at[i], send_sem=x_send.at[i], recv_sem=x_recv.at[i],
            device_id=(seq, lax.rem(head + i + 1, 4)), device_id_type=MESH,
        )
        for i in range(3)
    ]
    for x in xs:
        x.start()
    for x in xs:
        x.wait_recv()
    total = msg[...] + sums[0] + sums[1] + sums[2]
    inv = 1.0 / jnp.sqrt(total[0:1] / ROW_WIDTH + EPS)
    fac = inv * inv * inv * total[1:2] / ROW_WIDTH
    both = jnp.transpose(jnp.where(rows == 0, inv, jnp.where(rows == 1, fac, 0.0)))
    inv_col, fac_col = both[:, 0:1], both[:, 1:2]

    def make_grad(h):
        ag = (inv_col * gh[h].astype(F32) - att[h] * fac_col).astype(BF16)
        agr[h] = ag
        put_state(1, h, mm(qh[h], ag, 0, 0))

    def query_side():
        def body(h):
            ag = agr[h]
            m = jnp.where(causal, mm(ag, vh[h], 1, 1), 0.0).astype(BF16)
            flat_a[pl.ds(h, TOK, stride=NH), :] = mm(m, kh[h], 1, 0) + mm(ag, prior[h], 1, 1)
            flat_b[pl.ds(h, TOK, stride=NH), :] = att[h] * inv_col
            kg_acc[h] = mm(m, qh[h], 0, 0)
            vg_acc[h] = mm(wts[h], ag, 0, 0)

        over(NH, body)

    stores = [
        pltpu.make_async_copy(src, dst, store_sem.at[i])
        for i, (src, dst) in enumerate(
            ((n_vm, n_out), (qg_vm, qg_out), (kg_vm, kg_out), (vg_vm, vg_out))
        )
    ]

    def emit(i, flat, ref):
        ref[...] = flat[...].reshape(TOK, NH, DH).astype(BF16)
        stores[i].start()

    def write_two():
        emit(0, flat_b, n_vm)
        emit(1, flat_a, qg_vm)

    out1, back1 = scan(
        1,
        lambda: over(HALF, lambda i: make_grad(oc * HALF + i)),
        lambda: over(HALF, lambda i: make_grad(c * HALF + i)),
        query_side,
        write_two,
        True,
    )

    def finish(h, lt):
        flat_a[pl.ds(h, TOK, stride=NH), :] = kg_acc[h] + mm(vh[h], lt, 1, 1)
        flat_b[pl.ds(h, TOK, stride=NH), :] = vg_acc[h] + mm(kh[h], lt, 1, 0)

    over(HALF, lambda i: finish(c * HALF + i, head_of(base, 1, i)))
    back1.wait_recv()
    over(HALF, lambda i: finish(oc * HALF + i, head_of(other, 1, i)))
    emit(2, flat_a, kg_vm)
    emit(3, flat_b, vg_vm)

    scan_end(0, out0, back0)
    scan_end(1, out1, back1)
    for x in xs:
        x.wait_send()
    for st in stores:
        st.wait()


def shards(queries, keys, values, out_grad):
    shape = (TOK, NH, DH)
    half = (CHIPS, ROWS, DH)
    vm = pltpu.VMEM
    dma = pltpu.SemaphoreType.DMA
    hm = (NH, TOK, DH)
    return pl.pallas_call(
        kernel,
        out_shape=[jax.ShapeDtypeStruct(shape, BF16)] * 4,
        in_specs=[pl.BlockSpec(memory_space=pl.ANY)] * 4,
        out_specs=[pl.BlockSpec(memory_space=pl.ANY)] * 4,
        scratch_shapes=[vm(shape, BF16)] * 8
        + [vm((TOK * NH, DH), F32)] * 2
        + [vm(hm, BF16)] * 5
        + [vm(hm, F32), vm(hm, BF16), vm(hm, BF16), vm(hm, F32), vm(hm, F32)]
        + [vm((2, 2 * CHIPS, ROWS, DH), F32)]
        + [vm((2,) + half, F32)] * 7
        + [vm((2, TOK, DH), F32), vm((8, TOK), F32), vm((3, 8, TOK), F32)]
        + [dma((4,)), dma((4,)), dma((4,)), dma((4,)), dma((4,)), dma((4,)), dma((3,)), dma((3,))],
        compiler_params=pltpu.CompilerParams(
            collective_id=0, has_side_effects=True, vmem_limit_bytes=48 << 20
        ),
    )(queries, keys, values, out_grad)


def solution(mesh):
    spec = P("seq", "head", None)
    return jax.shard_map(
        shards, mesh=mesh, in_specs=(spec,) * 4, out_specs=(spec,) * 4, check_vma=False
    )
```

time: 769 us -> 91.1 us (0.12)
  waiting for transfers between devices: 457 us -> 0 us
  other arithmetic: 204 us -> 0 us
  Pallas kernels: 0 us -> 82.8 us
  local copies, waits for them, and re-layouts: 54.5 us -> 7.33 us
  matrix products: 22.5 us -> 0 us
  between operations: 14.2 us -> 0.65 us
  blocking collectives: 8.37 us -> 0 us
    all_gather x2 -> x0, waiting for transfers between devices: 457 us -> none  [prefix(): pieces = lax.all_gather(value, axis)]
    select_n x126 -> x0, other arithmetic: 200 us -> none  [step(): return jnp.where(position < mine, longer, running)]
    pallas_call x0 -> x1, Pallas kernels: none -> 82.8 us  [shards(): pl.pallas_call(kernel, out_shape=[jax.ShapeDtypeStruct(shape, BF16)] * 4,...]
    rev x1 -> x0, local copies, waits for them, and re-layouts: 43.9 us -> none  [prefix(): pieces = pieces[::-1]]
    dot_general x12 -> x0, matrix products: 22.5 us -> none  [batched(): lax.dot_general(left, right, (((left_contract,), (right_contract,)), ((0,...]
    psum x1 -> x0, blocking collectives: 8.37 us -> none  [shards(): lax.psum((jnp.sum(attended * attended, axis=(0, 2)), jnp.sum(grad_hm * at...]
  transfers between devices with their start and end apart: 2 -> 0, of which waited for: 2 -> 0; matrix products, arithmetic and copies ran while one was open for 2% -> 0% of each run, Pallas kernels for 0% -> 0%
where the time goes in v1:
time: 91.1 us; the launch traced here: 90.8 us
  Pallas kernels  82.8 us (91%)
  local copies, waits for them, and re-layouts  7.33 us (8%)
    pallas_call x1, Pallas kernels, shards(): pl.pallas_call(kernel, out_shape=[jax.ShapeDtypeStruct(shape, BF16)] * 4,...  82.8 us
    unnamed x12, local copies, waits for them, and re-layouts  7.33 us

profile of v1, /device:TPU:1, one launch (start us, length us, event | category | flops | bytes accessed | tf_op | source)
XLA Modules:
  0.0 90.8 jit_solution(10712157513837227559)
XLA Ops:
  0.6 0.0 copy-start
  0.6 1.0 %copy-done = bf16[128,16,128]{2,1,0:T(8,128)(2,1)S(1)} copy-done((bf16[128,16,128]{2,1,0:T(8,128)(2,1)S(1)}, bf16[128,16,128]{2,1,0:T(8,128)(2,1)}, u32[]{:S(2)}) %copy-start) | copy-done | bytes 524312
  1.7 0.0 copy-start.1
  1.7 1.0 %copy-done.1 = bf16[128,16,128]{2,1,0:T(8,128)(2,1)S(1)} copy-done((bf16[128,16,128]{2,1,0:T(8,128)(2,1)S(1)}, bf16[128,16,128]{2,1,0:T(8,128)(2,1)}, u32[]{:S(2)}) %copy-start.1) | copy-done | bytes 524312
  2.7 0.0 copy-start.2
  2.7 1.0 %copy-done.2 = bf16[128,16,128]{2,1,0:T(8,128)(2,1)S(1)} copy-done((bf16[128,16,128]{2,1,0:T(8,128)(2,1)S(1)}, bf16[128,16,128]{2,1,0:T(8,128)(2,1)}, u32[]{:S(2)}) %copy-start.2) | copy-done | bytes 524312
  3.8 0.0 copy-start.3
  3.8 1.0 %copy-done.3 = bf16[128,16,128]{2,1,0:T(8,128)(2,1)S(1)} copy-done((bf16[128,16,128]{2,1,0:T(8,128)(2,1)S(1)}, bf16[128,16,128]{2,1,0:T(8,128)(2,1)}, u32[]{:S(2)}) %copy-start.3) | copy-done | bytes 524312
  4.8 82.8 %shard_map.75 = (bf16[128,16,128]{2,1,0:T(8,128)(2,1)S(1)}, bf16[128,16,128]{2,1,0:T(8,128)(2,1)S(1)}, bf16[128,16,128]{2,1,0:T(8,128)(2,1)S(1)}, bf16[128,16,128]{2,1,0:T(8,128)(2,1)S(1)}) custom-call(bf16[128,16,128]{2,1,0:T(8,128)(2,1)S(1)} %copy-done, bf16[128,16,128]{2,1,0:T(8,128)(2,1)S(1)} %copy-done.1, bf16[128,16,128]{2,1,0:T(8,128)(2,1)S(1)} %copy-done.2, ...), custom_call_target="tpu_custom_call" | custom-call | tf_op jit(solution)/shard_map/pallas_call | solution.py:283
  87.6 0.8 copy.12
  88.4 0.8 copy.13
  89.2 0.8 copy.14
  90.0 0.8 copy.15
Async XLA Ops:
  0.6 1.0 %copy-start = (bf16[128,16,128]{2,1,0:T(8,128)(2,1)S(1)}, bf16[128,16,128]{2,1,0:T(8,128)(2,1)}, u32[]{:S(2)}) copy-start(bf16[128,16,128]{2,1,0:T(8,128)(2,1)} %q_hbm.1) | copy-start | bytes 1572868
  1.7 1.0 %copy-start.1 = (bf16[128,16,128]{2,1,0:T(8,128)(2,1)S(1)}, bf16[128,16,128]{2,1,0:T(8,128)(2,1)}, u32[]{:S(2)}) copy-start(bf16[128,16,128]{2,1,0:T(8,128)(2,1)} %k_hbm.1) | copy-start | bytes 1572868
  2.7 1.0 %copy-start.2 = (bf16[128,16,128]{2,1,0:T(8,128)(2,1)S(1)}, bf16[128,16,128]{2,1,0:T(8,128)(2,1)}, u32[]{:S(2)}) copy-start(bf16[128,16,128]{2,1,0:T(8,128)(2,1)} %v_hbm.1) | copy-start | bytes 1572868
  3.8 1.0 %copy-start.3 = (bf16[128,16,128]{2,1,0:T(8,128)(2,1)S(1)}, bf16[128,16,128]{2,1,0:T(8,128)(2,1)}, u32[]{:S(2)}) copy-start(bf16[128,16,128]{2,1,0:T(8,128)(2,1)} %g_hbm.1) | copy-start | bytes 1572868

commit v2 on v1

v2 whole, which is shorter than its diff:
```python
import jax
import jax.numpy as jnp
from jax import lax
from jax.experimental import pallas as pl
from jax.experimental.pallas import tpu as pltpu
from jax.sharding import PartitionSpec as P

EPS = 1e-06
DELIVER = 4
CHIPS = 32
TOK = 128
NH = 16
DH = 128
HALF = NH // 2
CHUNKS = 2
CH = HALF // CHUNKS
ROWS = CH * DH // CHIPS
SPLIT = DH // ROWS
ROW_WIDTH = 64 * DH
MESH = pl.DeviceIdType.MESH
F32 = jnp.float32
BF16 = jnp.bfloat16


def mm(left, right, lc, rc):
    return lax.dot_general(
        left, right, (((lc,), (rc,)), ((), ())), preferred_element_type=F32
    )


def kernel(
    q_hbm, k_hbm, v_hbm, g_hbm,
    n_out, qg_out, kg_out, vg_out,
    q_in, k_in, v_in, g_in, n_vm, qg_vm, kg_vm, vg_vm,
    flat_a, flat_b, qh, kh, vh, gh, wts, att, agr, prior, kg_acc, vg_acc,
    given, state, sib, chip, owned, bases, base, share, other,
    acc, msg, sums,
    load_sem, store_sem, d2d_send, d2d_recv, a2a_send, a2a_recv, x_send, x_recv,
):
    seq, head = lax.axis_index("seq"), lax.axis_index("head")
    s, c = seq // 2, lax.rem(seq, 2)
    oc = 1 - c

    bar = pltpu.get_barrier_semaphore()

    def greet(i, _):
        t = lax.rem(s + i, CHIPS)
        pl.semaphore_signal(bar, inc=1, device_id=(2 * t + c, head), device_id_type=MESH)
        return 0

    pl.semaphore_signal(bar, inc=1, device_id=(2 * s + oc, head), device_id_type=MESH)
    for i in range(1, 4):
        pl.semaphore_signal(
            bar, inc=1, device_id=(seq, lax.rem(head + i, 4)), device_id_type=MESH
        )
    lax.fori_loop(1, CHIPS, greet, 0)

    loads = [
        pltpu.make_async_copy(src, dst, load_sem.at[i])
        for i, (src, dst) in enumerate(
            ((k_hbm, k_in), (v_hbm, v_in), (q_hbm, q_in), (g_hbm, g_in))
        )
    ]
    for ld in loads:
        ld.start()

    def flatten(src, flat):
        flat[...] = src[...].astype(F32).reshape(TOK * NH, DH)

    def pick(flat, h):
        return flat[pl.ds(h, TOK, stride=NH), :].astype(BF16)

    def over(body):
        def step(i, _):
            for u in range(4):
                body(4 * i + u)
            return 0

        lax.fori_loop(0, NH // 4, step, 0)

    rows = lax.broadcasted_iota(jnp.int32, (TOK, TOK), 0)
    cols = lax.broadcasted_iota(jnp.int32, (TOK, TOK), 1)
    causal = cols <= rows

    def d2d(j, way, n, src, dst):
        return pltpu.make_async_remote_copy(
            src_ref=src.at[j, n], dst_ref=dst.at[j, n], send_sem=d2d_send.at[j, way, n],
            recv_sem=d2d_recv.at[j, way, n], device_id=(2 * s + oc, head), device_id_type=MESH,
        )

    def spread(j, way, n, src, dst):
        def send(i, _):
            t = lax.rem(s + i, CHIPS)
            pltpu.make_async_remote_copy(
                src_ref=src.at[j, n, t], dst_ref=dst.at[j, n, s],
                send_sem=a2a_send.at[j, way, n], recv_sem=a2a_recv.at[j, way, n],
                device_id=(2 * t + c, head), device_id_type=MESH,
            ).start()
            return 0

        lax.fori_loop(1, CHIPS, send, 0)
        dst[j, n, s] = src[j, n, s]

    def spread_all(j, way, n, src, dst):
        return pltpu.make_async_remote_copy(
            src_ref=src.at[j, n, pl.ds(0, CHIPS - 1)], dst_ref=dst.at[j, n, pl.ds(0, CHIPS - 1)],
            send_sem=a2a_send.at[j, way, n], recv_sem=a2a_recv.at[j, way, n],
            device_id=(2 * s + oc, head), device_id_type=MESH,
        )

    def put_state(ref, j, n, i, value):
        ref[j, n, pl.ds(i * SPLIT, SPLIT)] = value.reshape(SPLIT, ROWS, DH)

    def head_of(ref, j, n, i):
        return ref[j, n, pl.ds(i * SPLIT, SPLIT)].reshape(DH, DH).astype(BF16)

    def scan(j, make, during_up, during_down, use, reverse):
        for n in range(CHUNKS):
            for i in range(CH):
                put_state(given, j, n, i, make(oc * HALF + n * CH + i))
            if j == 0 and n == 0:
                pl.semaphore_wait(bar, CHIPS - 1 + 4)
            d2d(j, 0, n, given, sib).start()
            for i in range(CH):
                put_state(state, j, n, i, make(c * HALF + n * CH + i))
        for n in range(CHUNKS):
            d2d(j, 0, n, given, sib).wait_recv()
            chip[j, n] = state[j, n] + sib[j, n]
            spread(j, 0, n, chip, owned)
        during_up()
        for n in range(CHUNKS):
            spread_all(j, 0, n, chip, owned).wait_recv()
            run = jnp.zeros((ROWS, DH), F32)
            for t in range(CHIPS - 1, -1, -1) if reverse else range(CHIPS):
                bases[j, n, t] = run
                run = run + owned[j, n, t]
            spread(j, 1, n, bases, base)
        during_down()
        first = oc if reverse else c
        for n in range(CHUNKS):
            spread_all(j, 1, n, bases, base).wait_recv()
            share[j, n] = base[j, n] + jnp.where(first == 0, state[j, n], 0.0)
            d2d(j, 1, n, share, other).start()
            base[j, n] = base[j, n] + jnp.where(first == 1, sib[j, n], 0.0)
            for i in range(CH):
                use(c * HALF + n * CH + i, head_of(base, j, n, i))
        for n in range(CHUNKS):
            d2d(j, 1, n, share, other).wait_recv()
            for i in range(CH):
                use(oc * HALF + n * CH + i, head_of(other, j, n, i))

    def scan_end(j):
        for n in range(CHUNKS):
            d2d(j, 0, n, given, sib).wait_send()
            d2d(j, 1, n, share, other).wait_send()
            spread_all(j, 0, n, chip, owned).wait_send()
            spread_all(j, 1, n, bases, base).wait_send()

    loads[0].wait()
    flatten(k_in, flat_a)
    loads[1].wait()
    flatten(v_in, flat_b)

    def make_state(h):
        kk, vv = pick(flat_a, h), pick(flat_b, h)
        kh[h], vh[h] = kk, vv
        return mm(kk, vv, 0, 0)

    def local_attention():
        loads[2].wait()
        flatten(q_in, flat_a)

        def body(h):
            qq = pick(flat_a, h)
            qh[h] = qq
            w = jnp.where(causal, mm(qq, kh[h], 1, 1), 0.0).astype(BF16)
            wts[h] = w
            att[h] = mm(w, vh[h], 1, 0)

        over(body)

    def load_grads():
        loads[3].wait()
        flatten(g_in, flat_b)

        def body(h):
            gh[h] = pick(flat_b, h)

        over(body)
        acc[...] = jnp.zeros_like(acc)

    def attend(h, pr):
        prior[h] = pr
        a = att[h] + mm(qh[h], pr, 1, 0)
        att[h] = a
        acc[0] += a * a
        acc[1] += a * gh[h].astype(F32)

    scan(0, make_state, local_attention, load_grads, attend, False)

    sq = jnp.sum(acc[0], axis=1, keepdims=True)
    dt = jnp.sum(acc[1], axis=1, keepdims=True)
    packed = jnp.where(cols == 0, sq, jnp.where(cols == 1, dt, 0.0))
    msg[...] = jnp.transpose(packed)[0:8]
    xs = [
        pltpu.make_async_remote_copy(
            src_ref=msg, dst_ref=sums.at[i], send_sem=x_send.at[i], recv_sem=x_recv.at[i],
            device_id=(seq, lax.rem(head + i + 1, 4)), device_id_type=MESH,
        )
        for i in range(3)
    ]
    for x in xs:
        x.start()
    for x in xs:
        x.wait_recv()
    total = msg[...] + sums[0] + sums[1] + sums[2]
    inv = 1.0 / jnp.sqrt(total[0:1] / ROW_WIDTH + EPS)
    fac = inv * inv * inv * total[1:2] / ROW_WIDTH
    both = jnp.transpose(jnp.where(rows == 0, inv, jnp.where(rows == 1, fac, 0.0)))
    inv_col, fac_col = both[:, 0:1], both[:, 1:2]

    def make_grad(h):
        ag = (inv_col * gh[h].astype(F32) - att[h] * fac_col).astype(BF16)
        agr[h] = ag
        return mm(qh[h], ag, 0, 0)

    def query_side():
        def body(h):
            ag = agr[h]
            m = jnp.where(causal, mm(ag, vh[h], 1, 1), 0.0).astype(BF16)
            flat_a[pl.ds(h, TOK, stride=NH), :] = mm(m, kh[h], 1, 0) + mm(ag, prior[h], 1, 1)
            flat_b[pl.ds(h, TOK, stride=NH), :] = att[h] * inv_col
            kg_acc[h] = mm(m, qh[h], 0, 0)
            vg_acc[h] = mm(wts[h], ag, 0, 0)

        over(body)

    stores = [
        pltpu.make_async_copy(src, dst, store_sem.at[i])
        for i, (src, dst) in enumerate(
            ((n_vm, n_out), (qg_vm, qg_out), (kg_vm, kg_out), (vg_vm, vg_out))
        )
    ]

    def emit(i, flat, ref):
        ref[...] = flat[...].reshape(TOK, NH, DH).astype(BF16)
        stores[i].start()

    def write_two():
        emit(0, flat_b, n_vm)
        emit(1, flat_a, qg_vm)

    def finish(h, lt):
        flat_a[pl.ds(h, TOK, stride=NH), :] = kg_acc[h] + mm(vh[h], lt, 1, 1)
        flat_b[pl.ds(h, TOK, stride=NH), :] = vg_acc[h] + mm(kh[h], lt, 1, 0)

    scan(1, make_grad, query_side, write_two, finish, True)
    emit(2, flat_a, kg_vm)
    emit(3, flat_b, vg_vm)

    scan_end(0)
    scan_end(1)
    for x in xs:
        x.wait_send()
    for st in stores:
        st.wait()


def deliver(*refs):
    sem = refs[8]
    copies = [pltpu.make_async_copy(refs[i], refs[4 + i], sem.at[i]) for i in range(4)]
    for cp in copies:
        cp.start()
    for cp in copies:
        cp.wait()


def shards(queries, keys, values, out_grad):
    shape = (TOK, NH, DH)
    half = (2, CHUNKS, CHIPS, ROWS, DH)
    per = (2, 2, CHUNKS)
    vm = pltpu.VMEM
    dma = pltpu.SemaphoreType.DMA
    hm = (NH, TOK, DH)
    results = pl.pallas_call(
        kernel,
        out_shape=[jax.ShapeDtypeStruct(shape, BF16)] * 4,
        in_specs=[pl.BlockSpec(memory_space=pltpu.HBM)] * 4,
        out_specs=[pl.BlockSpec(memory_space=pl.ANY)] * 4,
        scratch_shapes=[vm(shape, BF16)] * 8
        + [vm((TOK * NH, DH), F32)] * 2
        + [vm(hm, BF16)] * 5
        + [vm(hm, F32), vm(hm, BF16), vm(hm, BF16), vm(hm, F32), vm(hm, F32)]
        + [vm(half, F32)] * 9
        + [vm((2, TOK, DH), F32), vm((8, TOK), F32), vm((3, 8, TOK), F32)]
        + [dma((4,)), dma((4,)), dma(per), dma(per), dma(per), dma(per), dma((3,)), dma((3,))],
        compiler_params=pltpu.CompilerParams(
            collective_id=0, has_side_effects=True, vmem_limit_bytes=48 << 20
        ),
    )(*[pltpu.with_memory_space_constraint(x, pltpu.HBM) for x in (queries, keys, values, out_grad)])
    block = pl.BlockSpec((TOK // DELIVER, NH, DH), lambda i: (i, 0, 0))
    return pl.pallas_call(
        deliver,
        out_shape=[jax.ShapeDtypeStruct(shape, BF16)] * 4,
        in_specs=[pl.BlockSpec(memory_space=pltpu.VMEM)] * 4,
        out_specs=[pl.BlockSpec(memory_space=pl.ANY)] * 4,
        scratch_shapes=[dma((4,))],
        compiler_params=pltpu.CompilerParams(vmem_limit_bytes=8 << 20),
    )(*results)


def solution(mesh):
    spec = P("seq", "head", None)
    return jax.shard_map(
        shards, mesh=mesh, in_specs=(spec,) * 4, out_specs=(spec,) * 4, check_vma=False
    )
```

time: 91.1 us -> 76.9 us (0.84)
  local copies, waits for them, and re-layouts: 7.33 us -> 0 us
  Pallas kernels: 82.8 us -> 76.1 us
    pallas_call x1, Pallas kernels: 82.8 us -> 74.8 us  [shards(): pl.pallas_call(kernel, out_shape=[jax.ShapeDtypeStruct(shape, BF16)] * 4,...]
    unnamed x12 -> x0, local copies, waits for them, and re-layouts: 7.33 us -> none
    pallas_call x0 -> x1, Pallas kernels: none -> 1.35 us  [shards(): pl.pallas_call(deliver, out_shape=[jax.ShapeDtypeStruct(shape, BF16)] * 4...]
where the time goes in v2:
time: 76.9 us; the launch traced here: 76.8 us
  Pallas kernels  76.1 us (99%)
    pallas_call x1, Pallas kernels, shards(): pl.pallas_call(kernel, out_shape=[jax.ShapeDtypeStruct(shape, BF16)] * 4,...  74.8 us

profile of v2, /device:TPU:1, one launch (start us, length us, event | category | flops | bytes accessed | tf_op | source)
XLA Modules:
  0.0 76.8 jit_solution(4192006503962516192)
XLA Ops:
  0.6 74.8 %shard_map.75 = (bf16[128,16,128]{2,1,0:T(8,128)(2,1)S(1)}, bf16[128,16,128]{2,1,0:T(8,128)(2,1)S(1)}, bf16[128,16,128]{2,1,0:T(8,128)(2,1)S(1)}, bf16[128,16,128]{2,1,0:T(8,128)(2,1)S(1)}) custom-call(bf16[128,16,128]{2,1,0:T(8,128)(2,1)} %q_hbm.1, bf16[128,16,128]{2,1,0:T(8,128)(2,1)} %k_hbm.1, bf16[128,16,128]{2,1,0:T(8,128)(2,1)} %v_hbm.1, ...), custom_call_target="tpu_custom_call" | custom-call | tf_op jit(solution)/shard_map/pallas_call | solution.py:285
  75.4 1.3 %shard_map.76 = (bf16[128,16,128]{2,1,0:T(8,128)(2,1)}, bf16[128,16,128]{2,1,0:T(8,128)(2,1)}, bf16[128,16,128]{2,1,0:T(8,128)(2,1)}, bf16[128,16,128]{2,1,0:T(8,128)(2,1)}) custom-call(bf16[128,16,128]{2,1,0:T(8,128)(2,1)S(1)} %get-tuple-element.8.refs_0_, bf16[128,16,128]{2,1,0:T(8,128)(2,1)S(1)} %get-tuple-element.9.refs_1_, ...), custom_call_target="tpu_custom_call" | custom-call | tf_op jit(solution)/shard_map/pallas_call | solution.py:302

commit v3 on v2

v3 whole, which is shorter than its diff:
```python
import jax
import jax.numpy as jnp
from jax import lax
from jax.experimental import pallas as pl
from jax.experimental.pallas import tpu as pltpu
from jax.sharding import PartitionSpec as P

EPS = 1e-06
DELIVER = 4
CHIPS = 32
NY, NZ = 4, 8
TOK = 128
NH = 16
DH = 128
HALF = NH // 2
CHUNKS = 4
CH = HALF // CHUNKS
ROWS = CH * DH // CHIPS
SPLIT = NZ // CH
ROW_WIDTH = 64 * DH
MESH = pl.DeviceIdType.MESH
F32 = jnp.float32
BF16 = jnp.bfloat16


def mm(left, right, lc, rc):
    return lax.dot_general(
        left, right, (((lc,), (rc,)), ((), ())), preferred_element_type=F32
    )


def kernel(
    q_hbm, k_hbm, v_hbm, g_hbm,
    n_out, qg_out, kg_out, vg_out,
    q_in, k_in, v_in, g_in,
    flat_a, flat_b, qh, kh, vh, gh, wts, att, full, agr, prior, kg_acc, vg_acc,
    given, state, sib, share, other, base,
    mine, theirs, got, joint, owned, bases, early, relay, lent,
    acc, msg, sums,
    load_sem, d2d_send, d2d_recv, pair_send, pair_recv, far_send, far_recv, x_send, x_recv,
):
    seq, head = lax.axis_index("seq"), lax.axis_index("head")
    s, c = seq // 2, lax.rem(seq, 2)
    oc = 1 - c

    loads = [
        pltpu.make_async_copy(src, dst, load_sem.at[i])
        for i, (src, dst) in enumerate(
            ((k_hbm, k_in), (v_hbm, v_in), (q_hbm, q_in), (g_hbm, g_in))
        )
    ]
    for ld in loads:
        ld.start()

    y, z = s // NZ, lax.rem(s, NZ)
    odd = lax.rem(z, 2)
    sign = 2 * odd - 1
    mate = z - sign

    def at(yy, zz):
        return ((yy * NZ + zz) * 2 + c, head)

    def ring(zz):
        return lax.rem(zz + NZ, NZ)

    bar = pltpu.get_barrier_semaphore()
    peers = [(2 * s + oc, head), at(y, mate)]
    peers += [(seq, lax.rem(head + i, 4)) for i in range(1, 4)]
    peers += [
        at(lax.rem(y + dy, NY), ring(z + sign * w))
        for w in (0, 1, 2, 3, -2)
        for dy in range(NY)
        if w or dy
    ]
    for peer in peers:
        pl.semaphore_signal(bar, inc=1, device_id=peer, device_id_type=MESH)

    def flatten(src, flat):
        flat[...] = src[...].astype(F32).reshape(TOK * NH, DH)

    def pick(flat, h):
        return flat[pl.ds(h, TOK, stride=NH), :].astype(BF16)

    def over(body):
        def step(i, _):
            body([4 * i + u for u in range(4)])
            return 0

        lax.fori_loop(0, NH // 4, step, 0)

    rows = lax.broadcasted_iota(jnp.int32, (TOK, TOK), 0)
    cols = lax.broadcasted_iota(jnp.int32, (TOK, TOK), 1)
    causal = cols <= rows

    def copy(sems, k, src, dst, to):
        return pltpu.make_async_remote_copy(
            src_ref=src, dst_ref=dst, send_sem=sems[0].at[k], recv_sem=sems[1].at[k],
            device_id=to, device_id_type=MESH,
        )

    d2d_sems, pair_sems, far_sems = (d2d_send, d2d_recv), (pair_send, pair_recv), (far_send, far_recv)

    def d2d_up(j, n):
        return copy(d2d_sems, (j, 0, n), given.at[j, n], sib.at[j, n], peers[0])

    def d2d_down(j, n, part):
        return copy(
            d2d_sems, (j, 1 + part, n), share.at[j, n, pl.ds(4 * part, 4)],
            other.at[j, n, pl.ds(4 * part, 4)], peers[0],
        )

    def pair_up(j, n):
        return copy(pair_sems, (j, 0, n), theirs.at[j, n], got.at[j, n], peers[1])

    def pair_down(j, n):
        return copy(pair_sems, (j, 1, n), relay.at[j, n], lent.at[j, n], peers[1])

    def far(j, way, n):
        return copy(
            far_sems, (j, way, n), joint.at[j, n, pl.ds(0, 15)], owned.at[j, n, pl.ds(0, 15)], peers[1]
        )

    FAR = [(w, dy) for w in (3, 2, 1, 0) for dy in (2, 1, 3, 0) if w or dy]

    def slot_z(f):
        return ring(z + sign * f) if f < 4 else ring(mate - sign * (f - 4))

    def slot_of(zo):
        t = ring(sign * (zo - z))
        return jnp.where(t < 4, t, 11 - t)

    def put_state(ref, j, n, i, value):
        ref[j, n, pl.ds(i * SPLIT, SPLIT)] = value.reshape(SPLIT, NY * ROWS, DH)

    def head_of(ref, j, n, i):
        blocks = [ref[j, n, slot_of(i * SPLIT + u)] for u in range(SPLIT)]
        return jnp.concatenate(blocks, axis=0).astype(BF16)

    def scan(j, make, during_up, during_down, use, reverse):
        def theirs_of(n):
            return [oc * HALF + n * CH + i for i in range(CH)]

        def own_of(n):
            return [c * HALF + n * CH + i for i in range(CH)]

        def give(n):
            made = make(theirs_of(n) + own_of(n))
            for i in range(CH):
                put_state(given, j, n, i, made[i])
                put_state(state, j, n, i, made[CH + i])
            if j == 0 and n == 0:
                pl.semaphore_wait(bar, len(peers))
            d2d_up(j, n).start()

        def send_pair(n):
            d2d_up(j, n).wait_recv()
            for f in range(NZ):
                zo = slot_z(f)
                total = (state[j, n, zo] + sib[j, n, zo]).reshape(NY, ROWS, DH)
                ref = mine if f < 4 else theirs
                ref[j, n, pl.ds(f % 4 * NY, NY)] = total
            pair_up(j, n).start()

        def send_up(n):
            pair_up(j, n).wait_recv()
            joint[j, n] = mine[j, n] + got[j, n]
            for w, dy in FAR:
                yo = lax.rem(y + dy, NY)
                copy(
                    far_sems, (j, 0, n), joint.at[j, n, w * NY + yo], owned.at[j, n, y * 4 + z // 2],
                    at(yo, ring(z + sign * w)),
                ).start()
            owned[j, n, y * 4 + z // 2] = joint[j, n, y]

        def send_down(n):
            far(j, 0, n).wait_recv()
            run = jnp.zeros((ROWS, DH), F32)
            for t in range(15, -1, -1) if reverse else range(16):
                bases[j, n, t] = run
                run = run + owned[j, n, t]
            for w, dy in FAR:
                yr = lax.rem(y + dy, NY)
                zr = ring(z + w - 2 * w * lax.rem(z + w, 2))
                copy(
                    far_sems, (j, 1, n), bases.at[j, n, yr * 4 + zr // 2], early.at[j, n, w * NY + y],
                    at(yr, zr),
                ).start()
            early[j, n, y] = bases[j, n, y * 4 + z // 2]

        chip_first = 1 - odd if reverse else odd
        first = oc if reverse else c

        def settle(n, part, values):
            for w in range(4):
                f = 4 * part + w
                zo = slot_z(f)
                value = values[w * NY : (w + 1) * NY].reshape(NY * ROWS, DH)
                share[j, n, f] = value + jnp.where(first == 0, state[j, n, zo], 0.0)
                base[j, n, f] = value + jnp.where(first == 1, sib[j, n, zo], 0.0)
            d2d_down(j, n, part).start()

        def send_mate(n):
            far(j, 1, n).wait_recv()
            before = early[j, n]
            relay[j, n] = before + jnp.where(chip_first == 0, mine[j, n], 0.0)
            pair_down(j, n).start()
            settle(n, 0, before + jnp.where(chip_first == 1, got[j, n], 0.0))

        def finish_chunk(n):
            heads, states = [], []
            if n < CHUNKS:
                pair_down(j, n).wait_recv()
                settle(n, 1, lent[j, n])
                heads += own_of(n)
                states += [head_of(base, j, n, i) for i in range(CH)]
            if n:
                d2d_down(j, n - 1, 0).wait_recv()
                d2d_down(j, n - 1, 1).wait_recv()
                heads += theirs_of(n - 1)
                states += [head_of(other, j, n - 1, i) for i in range(CH)]
            use(heads, states)

        for n in range(CHUNKS + 2):
            if n < CHUNKS:
                give(n)
            if 0 <= n - 1 < CHUNKS:
                send_pair(n - 1)
            if n >= 2:
                send_up(n - 2)
        during_up()
        for n in range(CHUNKS):
            send_down(n)
        during_down()
        for n in range(CHUNKS):
            send_mate(n)
        for n in range(CHUNKS + 1):
            finish_chunk(n)

    def scan_end(j):
        for n in range(CHUNKS):
            d2d_up(j, n).wait_send()
            d2d_down(j, n, 0).wait_send()
            d2d_down(j, n, 1).wait_send()
            pair_up(j, n).wait_send()
            pair_down(j, n).wait_send()
            far(j, 0, n).wait_send()
            far(j, 1, n).wait_send()

    loads[0].wait()
    flatten(k_in, flat_a)
    loads[1].wait()
    flatten(v_in, flat_b)

    def make_state(heads):
        kv = [(pick(flat_a, h), pick(flat_b, h)) for h in heads]
        for h, (kk, vv) in zip(heads, kv):
            kh[h], vh[h] = kk, vv
        return [mm(kk, vv, 0, 0) for kk, vv in kv]

    def local_attention():
        loads[2].wait()
        flatten(q_in, flat_a)

        def body(heads):
            qs = [pick(flat_a, h) for h in heads]
            ws = [jnp.where(causal, mm(qq, kh[h], 1, 1), 0.0).astype(BF16) for h, qq in zip(heads, qs)]
            outs = [mm(w, vh[h], 1, 0) for h, w in zip(heads, ws)]
            for h, qq, w, o in zip(heads, qs, ws, outs):
                qh[h] = qq
                wts[h] = w
                att[h] = o

        over(body)

    def load_grads():
        loads[3].wait()
        flatten(g_in, flat_b)

        def body(heads):
            gs = [pick(flat_b, h) for h in heads]
            for h, gg in zip(heads, gs):
                gh[h] = gg

        over(body)
        acc[...] = jnp.zeros_like(acc)

    def attend(heads, priors):
        parts = [att[h] + mm(qh[h], pr, 1, 0) for h, pr in zip(heads, priors)]
        grads = [gh[h].astype(F32) for h in heads]
        for h, pr, a in zip(heads, priors, parts):
            prior[h] = pr
            full[h] = a
        acc[0] += sum(a * a for a in parts)
        acc[1] += sum(a * g for a, g in zip(parts, grads))

    scan(0, make_state, local_attention, load_grads, attend, False)

    sq = jnp.sum(acc[0], axis=1, keepdims=True)
    dt = jnp.sum(acc[1], axis=1, keepdims=True)
    packed = jnp.where(cols == 0, sq, jnp.where(cols == 1, dt, 0.0))
    msg[...] = jnp.transpose(packed)[0:8]
    xs = [
        pltpu.make_async_remote_copy(
            src_ref=msg, dst_ref=sums.at[i], send_sem=x_send.at[i], recv_sem=x_recv.at[i],
            device_id=(seq, lax.rem(head + i + 1, 4)), device_id_type=MESH,
        )
        for i in range(3)
    ]
    for x in xs:
        x.start()
    for x in xs:
        x.wait_recv()
    total = msg[...] + sums[0] + sums[1] + sums[2]
    inv = 1.0 / jnp.sqrt(total[0:1] / ROW_WIDTH + EPS)
    fac = inv * inv * inv * total[1:2] / ROW_WIDTH
    both = jnp.transpose(jnp.where(rows == 0, inv, jnp.where(rows == 1, fac, 0.0)))
    inv_col, fac_col = both[:, 0:1], both[:, 1:2]

    def make_grad(heads):
        ags = [(inv_col * gh[h].astype(F32) - full[h] * fac_col).astype(BF16) for h in heads]
        for h, ag in zip(heads, ags):
            agr[h] = ag
        return [mm(qh[h], ag, 0, 0) for h, ag in zip(heads, ags)]

    def query_side():
        def body(heads):
            ags = [agr[h] for h in heads]
            ms = [jnp.where(causal, mm(ag, vh[h], 1, 1), 0.0).astype(BF16) for h, ag in zip(heads, ags)]
            qgs = [
                mm(m, kh[h], 1, 0) + mm(ag, prior[h], 1, 1) for h, m, ag in zip(heads, ms, ags)
            ]
            kgs = [mm(m, qh[h], 0, 0) for h, m in zip(heads, ms)]
            vgs = [mm(wts[h], ag, 0, 0) for h, ag in zip(heads, ags)]
            normed = [full[h] * inv_col for h in heads]
            for i, h in enumerate(heads):
                flat_a[pl.ds(h, TOK, stride=NH), :] = qgs[i]
                flat_b[pl.ds(h, TOK, stride=NH), :] = normed[i]
                kg_acc[h] = kgs[i]
                vg_acc[h] = vgs[i]

        over(body)

    def emit(flat, ref):
        ref[...] = flat[...].reshape(TOK, NH, DH).astype(BF16)

    def write_two():
        emit(flat_b, n_out)
        emit(flat_a, qg_out)

    def finish(heads, laters):
        keys = [kg_acc[h] + mm(vh[h], lt, 1, 1) for h, lt in zip(heads, laters)]
        values = [vg_acc[h] + mm(kh[h], lt, 1, 0) for h, lt in zip(heads, laters)]
        for h, kg, vg in zip(heads, keys, values):
            flat_a[pl.ds(h, TOK, stride=NH), :] = kg
            flat_b[pl.ds(h, TOK, stride=NH), :] = vg

    scan(1, make_grad, query_side, write_two, finish, True)
    emit(flat_a, kg_out)
    emit(flat_b, vg_out)

    scan_end(0)
    scan_end(1)
    for x in xs:
        x.wait_send()


def deliver(*refs):
    sem = refs[8]
    copies = [pltpu.make_async_copy(refs[i], refs[4 + i], sem.at[i]) for i in range(4)]
    for cp in copies:
        cp.start()
    for cp in copies:
        cp.wait()


def shards(queries, keys, values, out_grad):
    shape = (TOK, NH, DH)
    half = (2, CHUNKS, NZ, NY * ROWS, DH)
    part = (2, CHUNKS, 16, ROWS, DH)
    per = (2, 2, CHUNKS)
    vm = pltpu.VMEM
    dma = pltpu.SemaphoreType.DMA
    hm = (NH, TOK, DH)
    results = pl.pallas_call(
        kernel,
        out_shape=[jax.ShapeDtypeStruct(shape, BF16)] * 4,
        in_specs=[pl.BlockSpec(memory_space=pltpu.HBM)] * 4,
        out_specs=[pl.BlockSpec(memory_space=pltpu.VMEM)] * 4,
        scratch_shapes=[vm(shape, BF16)] * 4
        + [vm((TOK * NH, DH), F32)] * 2
        + [vm(hm, BF16)] * 5
        + [vm(hm, F32), vm(hm, F32), vm(hm, BF16), vm(hm, BF16), vm(hm, F32), vm(hm, F32)]
        + [vm(half, F32)] * 6
        + [vm(part, F32)] * 9
        + [vm((2, TOK, DH), F32), vm((8, TOK), F32), vm((3, 8, TOK), F32)]
        + [dma((4,)), dma((2, 3, CHUNKS)), dma((2, 3, CHUNKS)), dma(per), dma(per), dma(per), dma(per)]
        + [dma((3,)), dma((3,))],
        compiler_params=pltpu.CompilerParams(
            collective_id=0, has_side_effects=True, vmem_limit_bytes=48 << 20
        ),
    )(*[pltpu.with_memory_space_constraint(x, pltpu.HBM) for x in (queries, keys, values, out_grad)])
    block = pl.BlockSpec((TOK // DELIVER, NH, DH), lambda i: (i, 0, 0))
    return pl.pallas_call(
        deliver,
        out_shape=[jax.ShapeDtypeStruct(shape, BF16)] * 4,
        in_specs=[pl.BlockSpec(memory_space=pltpu.VMEM)] * 4,
        out_specs=[pl.BlockSpec(memory_space=pl.ANY)] * 4,
        scratch_shapes=[dma((4,))],
        compiler_params=pltpu.CompilerParams(vmem_limit_bytes=8 << 20),
    )(*results)


def solution(mesh):
    spec = P("seq", "head", None)
    return jax.shard_map(
        shards, mesh=mesh, in_specs=(spec,) * 4, out_specs=(spec,) * 4, check_vma=False
    )
```

time: 76.9 us -> 74.9 us (0.974)
  Pallas kernels: 76.1 us -> 74.2 us
    pallas_call x1, Pallas kernels: 74.8 us -> 72.9 us  [shards(): pl.pallas_call(kernel, out_shape=[jax.ShapeDtypeStruct(shape, BF16)] * 4,...]
where the time goes in v3:
time: 74.9 us; the launch traced here: 74.8 us
  Pallas kernels  74.2 us (99%)
    pallas_call x1, Pallas kernels, shards(): pl.pallas_call(kernel, out_shape=[jax.ShapeDtypeStruct(shape, BF16)] * 4,...  72.9 us

profile of v3, /device:TPU:1, one launch (start us, length us, event | category | flops | bytes accessed | tf_op | source)
XLA Modules:
  0.0 74.8 jit_solution(15483376385436656231)
XLA Ops:
  0.6 72.9 %shard_map.75 = (bf16[128,16,128]{2,1,0:T(8,128)(2,1)S(1)}, bf16[128,16,128]{2,1,0:T(8,128)(2,1)S(1)}, bf16[128,16,128]{2,1,0:T(8,128)(2,1)S(1)}, bf16[128,16,128]{2,1,0:T(8,128)(2,1)S(1)}) custom-call(bf16[128,16,128]{2,1,0:T(8,128)(2,1)} %q_hbm.1, bf16[128,16,128]{2,1,0:T(8,128)(2,1)} %k_hbm.1, bf16[128,16,128]{2,1,0:T(8,128)(2,1)} %v_hbm.1, ...), custom_call_target="tpu_custom_call" | custom-call | tf_op jit(solution)/shard_map/pallas_call | solution.py:384
  73.5 1.3 %shard_map.76 = (bf16[128,16,128]{2,1,0:T(8,128)(2,1)}, bf16[128,16,128]{2,1,0:T(8,128)(2,1)}, bf16[128,16,128]{2,1,0:T(8,128)(2,1)}, bf16[128,16,128]{2,1,0:T(8,128)(2,1)}) custom-call(bf16[128,16,128]{2,1,0:T(8,128)(2,1)S(1)} %get-tuple-element.8.refs_0_, bf16[128,16,128]{2,1,0:T(8,128)(2,1)S(1)} %get-tuple-element.9.refs_1_, ...), custom_call_target="tpu_custom_call" | custom-call | tf_op jit(solution)/shard_map/pallas_call | solution.py:403

commit v4 on v3

v4 whole, which is shorter than its diff:
```python
import jax
import jax.numpy as jnp
from jax import lax
from jax.experimental import pallas as pl
from jax.experimental.pallas import tpu as pltpu
from jax.sharding import PartitionSpec as P

EPS = 1e-06
CHIPS = 32
NY, NZ = 4, 8
TOK = 128
NH = 16
DH = 128
HALF = NH // 2
CHUNKS = 4
CH = HALF // CHUNKS
ROWS = CH * DH // CHIPS
SPLIT = NZ // CH
ROW_WIDTH = 64 * DH
MESH = pl.DeviceIdType.MESH
FORWARD_FILL = {"start": (0, 1), "down1": (2,), "down3": (3, 4, 5)}
BACKWARD_FILL = {"start": (0,), "down1": (1, 2), "down3": (3, 4), "mate3": (5,)}
F32 = jnp.float32
BF16 = jnp.bfloat16


def mm(left, right, lc, rc):
    return lax.dot_general(
        left, right, (((lc,), (rc,)), ((), ())), preferred_element_type=F32
    )


def kernel(
    q_hbm, k_hbm, v_hbm, g_hbm,
    n_out, qg_out, kg_out, vg_out,
    q_in, k_in, v_in, g_in,
    flat_a, flat_b, qh, kh, vh, gh, wts, agr, prior, att, full, kg_acc, vg_acc,
    lend, borrow, give_back, take_back, given, base, state,
    mine, theirs, got, joint, owned, bases, early, relay, lent,
    acc, msg, sums,
    load_sem, d2d_send, d2d_recv, pair_send, pair_recv, far_send, far_recv, x_send, x_recv,
):
    seq, head = lax.axis_index("seq"), lax.axis_index("head")
    s, c = seq // 2, lax.rem(seq, 2)
    oc = 1 - c

    loads = [
        pltpu.make_async_copy(src, dst, load_sem.at[i])
        for i, (src, dst) in enumerate(
            ((k_hbm, k_in), (v_hbm, v_in), (q_hbm, q_in), (g_hbm, g_in))
        )
    ]
    for ld in loads:
        ld.start()

    y, z = s // NZ, lax.rem(s, NZ)
    odd = lax.rem(z, 2)
    sign = 2 * odd - 1
    mate = z - sign

    def at(yy, zz):
        return ((yy * NZ + zz) * 2 + c, head)

    def ring(zz):
        return lax.rem(zz + NZ, NZ)

    bar = pltpu.get_barrier_semaphore()
    sibling, partner = (2 * s + oc, head), at(y, mate)
    sum_peers = [sibling] + [
        (2 * s + cc, lax.rem(head + i, 4)) for i in range(1, 4) for cc in (c, oc)
    ]
    peers = sum_peers + [partner]
    peers += [
        at(lax.rem(y + dy, NY), ring(z + sign * w))
        for w in (0, 1, 2, 3, -2)
        for dy in range(NY)
        if w or dy
    ]
    for peer in peers:
        pl.semaphore_signal(bar, inc=1, device_id=peer, device_id_type=MESH)

    def flatten(src, flat):
        flat[...] = src[...].astype(F32).reshape(TOK * NH, DH)

    def pick(flat, h):
        return flat[pl.ds(h, TOK, stride=NH), :]

    def place(flat, h, value):
        flat[pl.ds(h, TOK, stride=NH), :] = value

    def by_four(body):
        def step(i, _):
            body([4 * i + u for u in range(4)])
            return 0

        lax.fori_loop(0, HALF // 4, step, 0)

    rows = lax.broadcasted_iota(jnp.int32, (TOK, TOK), 0)
    cols = lax.broadcasted_iota(jnp.int32, (TOK, TOK), 1)
    causal = cols <= rows

    def copy(sems, k, src, dst, to):
        return pltpu.make_async_remote_copy(
            src_ref=src, dst_ref=dst, send_sem=sems[0].at[k], recv_sem=sems[1].at[k],
            device_id=to, device_id_type=MESH,
        )

    d2d_sems, pair_sems, far_sems = (d2d_send, d2d_recv), (pair_send, pair_recv), (far_send, far_recv)

    def state_swap(n):
        return copy(d2d_sems, n, given.at[n], state.at[0, c, n], sibling)

    def state_swap_wait(n):
        return copy(d2d_sems, n, given.at[n], state.at[0, oc, n], sibling)

    def lending(i):
        return copy(d2d_sems, CHUNKS + i, lend.at[i], borrow.at[i], sibling)

    def returning(i):
        return copy(d2d_sems, CHUNKS + 4 + i, give_back.at[i], take_back.at[i], sibling)

    def returning_part(i, n):
        part = pl.ds(n * CH, CH)
        return copy(
            d2d_sems, CHUNKS + 4 + 2 * (n + 1) + i - 2, give_back.at[i, part], take_back.at[i, part], sibling
        )

    def pair_up(j, n):
        return copy(pair_sems, (j, 0, n), theirs.at[j, n], got.at[j, n], partner)

    def pair_down(j, n):
        return copy(pair_sems, (j, 1, n), relay.at[j, n], lent.at[j, n], partner)

    def far(j, way, n):
        return copy(
            far_sems, (j, way, n), joint.at[j, n, pl.ds(0, 15)], owned.at[j, n, pl.ds(0, 15)], partner
        )

    FAR = [(w, dy) for w in (3, 2, 1, 0) for dy in (2, 1, 3, 0) if w or dy]

    def slot_z(f):
        return ring(z + sign * f) if f < 4 else ring(mate - sign * (f - 4))

    def slot_of(zo):
        t = ring(sign * (zo - z))
        return jnp.where(t < 4, t, 11 - t)

    def cut(value):
        return value.reshape(SPLIT, NY * ROWS, DH)

    def state_of(j, b, n, i):
        return state[j, b, n, pl.ds(i * SPLIT, SPLIT)].reshape(DH, DH)

    def base_of(n, i):
        return jnp.concatenate([base[n, slot_of(i * SPLIT + u)] for u in range(SPLIT)], axis=0)

    def scan(j, make, fill, use, reverse):
        def send_pair(n):
            if j == 0:
                state_swap_wait(n).wait_recv()
            for f in range(NZ):
                zo = slot_z(f)
                total = (state[j, 0, n, zo] + state[j, 1, n, zo]).reshape(NY, ROWS, DH)
                ref = mine if f < 4 else theirs
                ref[j, n, pl.ds(f % 4 * NY, NY)] = total
            pair_up(j, n).start()

        def send_up(n):
            pair_up(j, n).wait_recv()
            joint[j, n] = mine[j, n] + got[j, n]
            for w, dy in FAR:
                yo = lax.rem(y + dy, NY)
                copy(
                    far_sems, (j, 0, n), joint.at[j, n, w * NY + yo], owned.at[j, n, y * 4 + z // 2],
                    at(yo, ring(z + sign * w)),
                ).start()
            owned[j, n, y * 4 + z // 2] = joint[j, n, y]

        def send_down(n):
            far(j, 0, n).wait_recv()
            run = jnp.zeros((ROWS, DH), F32)
            for t in range(15, -1, -1) if reverse else range(16):
                bases[j, n, t] = run
                run = run + owned[j, n, t]
            for w, dy in FAR:
                yr = lax.rem(y + dy, NY)
                zr = ring(z + w - 2 * w * lax.rem(z + w, 2))
                copy(
                    far_sems, (j, 1, n), bases.at[j, n, yr * 4 + zr // 2], early.at[j, n, w * NY + y],
                    at(yr, zr),
                ).start()
            early[j, n, y] = bases[j, n, y * 4 + z // 2]

        chip_first = 1 - odd if reverse else odd

        def send_mate(n):
            far(j, 1, n).wait_recv()
            before = early[j, n]
            relay[j, n] = before + jnp.where(chip_first == 0, mine[j, n], 0.0)
            pair_down(j, n).start()
            own = before + jnp.where(chip_first == 1, got[j, n], 0.0)
            base[n, pl.ds(0, 4)] = own.reshape(4, NY * ROWS, DH)

        def finish_chunk(n):
            pair_down(j, n).wait_recv()
            base[n, pl.ds(4, 4)] = lent[j, n].reshape(4, NY * ROWS, DH)
            heads = [n * CH + i for i in range(CH)]
            first = [base_of(n, i) for i in range(CH)]
            block = 1 if reverse else 0
            second = [f + state_of(j, block, n, i) for i, f in enumerate(first)]
            first, second = [[x.astype(BF16) for x in xs] for xs in (first, second)]
            use(n, heads, *((second, first) if reverse else (first, second)))

        for n in range(CHUNKS + 2):
            if n < CHUNKS:
                make(n)
            if 0 <= n - 1 < CHUNKS:
                send_pair(n - 1)
            if n >= 2:
                send_up(n - 2)
        fill("start")
        for n in range(CHUNKS):
            send_down(n)
            fill("down%d" % n)
        for n in range(CHUNKS):
            send_mate(n)
            fill("mate%d" % n)
        for n in range(CHUNKS):
            finish_chunk(n)

    def scan_end(j):
        for n in range(CHUNKS):
            pair_up(j, n).wait_send()
            pair_down(j, n).wait_send()
            far(j, 0, n).wait_send()
            far(j, 1, n).wait_send()

    loads[0].wait()
    flatten(k_in, flat_a)
    loads[1].wait()
    flatten(v_in, flat_b)

    def make_state(n):
        span = range(n * CH, n * CH + CH)
        away = [(pick(flat_a, oc * HALF + i), pick(flat_b, oc * HALF + i)) for i in span]
        here = [(pick(flat_a, c * HALF + i), pick(flat_b, c * HALF + i)) for i in span]
        states = [mm(kk.astype(BF16), vv.astype(BF16), 0, 0) for kk, vv in away + here]
        for u, i in enumerate(span):
            lend[0, i], lend[1, i] = away[u]
            kk, vv = here[u]
            kh[c * HALF + i] = kk.astype(BF16)
            vh[c * HALF + i] = vv.astype(BF16)
            given[n, pl.ds(u * SPLIT, SPLIT)] = cut(states[u])
            state[0, c, n, pl.ds(u * SPLIT, SPLIT)] = cut(states[CH + u])
        if n == 0:
            pl.semaphore_wait(bar, len(peers))
        state_swap(n).start()

    def share(index, flat, ref):
        def body(heads):
            away = [pick(flat, oc * HALF + i) for i in heads]
            here = [pick(flat, c * HALF + i).astype(BF16) for i in heads]
            for i, x, m in zip(heads, away, here):
                lend[index, i] = x
                ref[c * HALF + i] = m

        by_four(body)
        lending(index).start()

    def receive(index, ref):
        lending(index).wait_recv()

        def body(heads):
            for i in heads:
                ref[oc * HALF + i] = borrow[index, i].astype(BF16)

        by_four(body)

    def local_attention(b):
        def body(heads):
            hs = [b * HALF + i for i in heads]
            ws = [jnp.where(causal, mm(qh[h], kh[h], 1, 1), 0.0).astype(BF16) for h in hs]
            outs = [mm(w, vh[h], 1, 0) for h, w in zip(hs, ws)]
            for h, w, o in zip(hs, ws, outs):
                wts[h] = w
                att[h] = o

        by_four(body)

    def lend_query():
        lending(0).start()
        lending(1).start()
        loads[2].wait()
        flatten(q_in, flat_a)
        share(2, flat_a, qh)

    def lend_grad():
        loads[3].wait()
        flatten(g_in, flat_b)
        share(3, flat_b, gh)

    def borrow_three():
        receive(0, kh)
        receive(1, vh)
        receive(2, qh)

    def borrow_grad():
        receive(3, gh)
        acc[...] = jnp.zeros_like(acc)

    forward_work = [
        lend_query, lend_grad, lambda: local_attention(c), borrow_three, lambda: local_attention(oc),
        borrow_grad,
    ]

    def fill_forward(place_name):
        for task in FORWARD_FILL.get(place_name, ()):
            forward_work[task]()

    def attend(n, heads, *priors):
        for b in range(2):
            hs = [b * HALF + i for i in heads]
            parts = [att[h] + mm(qh[h], pr, 1, 0) for h, pr in zip(hs, priors[b])]
            grads = [gh[h].astype(F32) for h in hs]
            for h, pr, a in zip(hs, priors[b], parts):
                prior[h] = pr
                full[h] = a
            acc[b, 0] += sum(a * a for a in parts)
            acc[b, 1] += sum(a * g for a, g in zip(parts, grads))

    scan(0, make_state, fill_forward, attend, False)

    packed = jnp.zeros((TOK, TOK), F32)
    for b in range(2):
        for i in range(2):
            packed = jnp.where(cols == 2 * b + i, jnp.sum(acc[b, i], axis=1, keepdims=True), packed)
    msg[...] = jnp.transpose(packed)[0:8]
    xs = [
        copy((x_send, x_recv), i, msg, sums.at[i], peer) for i, peer in enumerate(sum_peers)
    ]
    for x in xs:
        x.start()
    for x in xs:
        x.wait_recv()
    total = msg[...]
    for i in range(len(xs)):
        total = total + sums[i]
    back = jnp.zeros((TOK, TOK), F32)
    for b in range(2):
        inv = 1.0 / jnp.sqrt(total[2 * b : 2 * b + 1] / ROW_WIDTH + EPS)
        fac = inv * inv * inv * total[2 * b + 1 : 2 * b + 2] / ROW_WIDTH
        back = jnp.where(rows == 2 * b, inv, jnp.where(rows == 2 * b + 1, fac, back))
    back = jnp.transpose(back)
    inv_col = [back[:, 0:1], back[:, 2:3]]
    fac_col = [back[:, 1:2], back[:, 3:4]]

    def make_grad(n):
        span = range(n * CH, n * CH + CH)
        where = [(b, u, b * HALF + i) for b in range(2) for u, i in enumerate(span)]
        ags = [
            (inv_col[b] * gh[h].astype(F32) - full[h] * fac_col[b]).astype(BF16) for b, _, h in where
        ]
        states = [mm(qh[h], ag, 0, 0) for (_, _, h), ag in zip(where, ags)]
        for (b, u, h), ag, st in zip(where, ags, states):
            agr[h] = ag
            state[1, b, n, pl.ds(u * SPLIT, SPLIT)] = cut(st)

    def query_side(b, start, keep):
        scale = jnp.where(b == 0, inv_col[0], inv_col[1])

        def body(heads):
            hs = [b * HALF + i for i in heads]
            ags = [agr[h] for h in hs]
            ms = [jnp.where(causal, mm(ag, vh[h], 1, 1), 0.0).astype(BF16) for h, ag in zip(hs, ags)]
            qgs = [mm(m, kh[h], 1, 0) + mm(ag, prior[h], 1, 1) for h, m, ag in zip(hs, ms, ags)]
            kgs = [mm(m, qh[h], 0, 0) for h, m in zip(hs, ms)]
            vgs = [mm(wts[h], ag, 0, 0) for h, ag in zip(hs, ags)]
            normed = [full[h] * scale for h in hs]
            for u, i in enumerate(heads):
                keep(i, normed[u], qgs[u])
                kg_acc[hs[u]] = kgs[u]
                vg_acc[hs[u]] = vgs[u]

        body([start + u for u in range(4)])

    def keep_away(i, left, right):
        give_back[0, i] = left
        give_back[1, i] = right

    def keep_here(i, left, right):
        place(flat_a, c * HALF + i, left)
        place(flat_b, c * HALF + i, right)

    def emit(flat, ref):
        ref[...] = flat[...].reshape(TOK, NH, DH).astype(BF16)

    def give_two():
        returning(0).start()
        returning(1).start()

    def write_two():
        returning(0).wait_recv()
        returning(1).wait_recv()

        def body(heads):
            for i in heads:
                place(flat_a, oc * HALF + i, take_back[0, i])
                place(flat_b, oc * HALF + i, take_back[1, i])

        by_four(body)
        emit(flat_a, n_out)
        emit(flat_b, qg_out)

    backward_work = [
        lambda: query_side(oc, 0, keep_away), lambda: query_side(oc, 4, keep_away), give_two,
        lambda: query_side(c, 0, keep_here), lambda: query_side(c, 4, keep_here), write_two,
    ]

    def fill_backward(place_name):
        for task in BACKWARD_FILL.get(place_name, ()):
            backward_work[task]()

    def collect(n):
        for i in range(2):
            returning_part(2 + i, n).wait_recv()
        for i in range(n * CH, n * CH + CH):
            place(flat_a, oc * HALF + i, take_back[2, i])
            place(flat_b, oc * HALF + i, take_back[3, i])

    def finish(n, heads, *laters):
        def grads(b):
            hs = [b * HALF + i for i in heads]
            lts = [jnp.where(b == 0, l0, l1) for l0, l1 in zip(*laters)]
            keys = [kg_acc[h] + mm(vh[h], lt, 1, 1) for h, lt in zip(hs, lts)]
            values = [vg_acc[h] + mm(kh[h], lt, 1, 0) for h, lt in zip(hs, lts)]
            return keys, values

        for i, kg, vg in zip(heads, *grads(oc)):
            give_back[2, i] = kg
            give_back[3, i] = vg
        for i in range(2):
            returning_part(2 + i, n).start()
        for i, kg, vg in zip(heads, *grads(c)):
            keep_here(i, kg, vg)
        if n:
            collect(n - 1)

    scan(1, make_grad, fill_backward, finish, True)
    collect(CHUNKS - 1)
    emit(flat_a, kg_out)
    emit(flat_b, vg_out)

    for n in range(CHUNKS):
        state_swap(n).wait_send()
        for i in range(2):
            returning_part(2 + i, n).wait_send()
    for i in range(4):
        lending(i).wait_send()
    for i in range(2):
        returning(i).wait_send()
    scan_end(0)
    scan_end(1)
    for x in xs:
        x.wait_send()


def deliver(*refs):
    sem = refs[8]
    copies = [pltpu.make_async_copy(refs[i], refs[4 + i], sem.at[i]) for i in range(4)]
    for cp in copies:
        cp.start()
    for cp in copies:
        cp.wait()


def shards(queries, keys, values, out_grad):
    shape = (TOK, NH, DH)
    half = (CHUNKS, NZ, NY * ROWS, DH)
    part = (2, CHUNKS, 16, ROWS, DH)
    per = (2, 2, CHUNKS)
    vm = pltpu.VMEM
    dma = pltpu.SemaphoreType.DMA
    hm = (NH, TOK, DH)
    swap = (4, HALF, TOK, DH)
    d2d = 4 + 4 + 3 * CHUNKS
    results = pl.pallas_call(
        kernel,
        out_shape=[jax.ShapeDtypeStruct(shape, BF16)] * 4,
        in_specs=[pl.BlockSpec(memory_space=pltpu.HBM)] * 4,
        out_specs=[pl.BlockSpec(memory_space=pltpu.VMEM)] * 4,
        scratch_shapes=[vm(shape, BF16)] * 4
        + [vm((TOK * NH, DH), F32)] * 2
        + [vm(hm, BF16)] * 7
        + [vm(hm, F32)] * 4
        + [vm(swap, F32)] * 4
        + [vm(half, F32)] * 2
        + [vm((2, 2) + half, F32)]
        + [vm(part, F32)] * 9
        + [vm((2, 2, TOK, DH), F32), vm((8, TOK), F32), vm((7, 8, TOK), F32)]
        + [dma((4,)), dma((d2d,)), dma((d2d,)), dma(per), dma(per), dma(per), dma(per)]
        + [dma((7,)), dma((7,))],
        compiler_params=pltpu.CompilerParams(
            collective_id=0, has_side_effects=True, vmem_limit_bytes=48 << 20
        ),
    )(*[pltpu.with_memory_space_constraint(x, pltpu.HBM) for x in (queries, keys, values, out_grad)])
    return pl.pallas_call(
        deliver,
        out_shape=[jax.ShapeDtypeStruct(shape, BF16)] * 4,
        in_specs=[pl.BlockSpec(memory_space=pltpu.VMEM)] * 4,
        out_specs=[pl.BlockSpec(memory_space=pl.ANY)] * 4,
        scratch_shapes=[dma((4,))],
        compiler_params=pltpu.CompilerParams(vmem_limit_bytes=8 << 20),
    )(*results)


def solution(mesh):
    spec = P("seq", "head", None)
    return jax.shard_map(
        shards, mesh=mesh, in_specs=(spec,) * 4, out_specs=(spec,) * 4, check_vma=False
    )
```

time: 74.9 us -> 72.4 us (0.967)
  Pallas kernels: 74.2 us -> 71.7 us
    pallas_call x1, Pallas kernels: 72.9 us -> 70.3 us  [shards(): pl.pallas_call(kernel, out_shape=[jax.ShapeDtypeStruct(shape, BF16)] * 4,...]
where the time goes in v4:
time: 72.4 us; the launch traced here: 72.3 us
  Pallas kernels  71.7 us (99%)
    pallas_call x1, Pallas kernels, shards(): pl.pallas_call(kernel, out_shape=[jax.ShapeDtypeStruct(shape, BF16)] * 4,...  70.3 us

profile of v4, /device:TPU:1, one launch (start us, length us, event | category | flops | bytes accessed | tf_op | source)
XLA Modules:
  0.0 72.3 jit_solution(12312321353457790471)
XLA Ops:
  0.6 70.3 %shard_map.75 = (bf16[128,16,128]{2,1,0:T(8,128)(2,1)S(1)}, bf16[128,16,128]{2,1,0:T(8,128)(2,1)S(1)}, bf16[128,16,128]{2,1,0:T(8,128)(2,1)S(1)}, bf16[128,16,128]{2,1,0:T(8,128)(2,1)S(1)}) custom-call(bf16[128,16,128]{2,1,0:T(8,128)(2,1)} %q_hbm.1, bf16[128,16,128]{2,1,0:T(8,128)(2,1)} %k_hbm.1, bf16[128,16,128]{2,1,0:T(8,128)(2,1)} %v_hbm.1, ...), custom_call_target="tpu_custom_call" | custom-call | tf_op jit(solution)/shard_map/pallas_call | solution.py:486
  71.0 1.3 %shard_map.76 = (bf16[128,16,128]{2,1,0:T(8,128)(2,1)}, bf16[128,16,128]{2,1,0:T(8,128)(2,1)}, bf16[128,16,128]{2,1,0:T(8,128)(2,1)}, bf16[128,16,128]{2,1,0:T(8,128)(2,1)}) custom-call(bf16[128,16,128]{2,1,0:T(8,128)(2,1)S(1)} %get-tuple-element.8.refs_0_, bf16[128,16,128]{2,1,0:T(8,128)(2,1)S(1)} %get-tuple-element.9.refs_1_, ...), custom_call_target="tpu_custom_call" | custom-call | tf_op jit(solution)/shard_map/pallas_call | solution.py:506

commit v5 on v4

--- a/solution.py
+++ b/solution.py
@@ -19,7 +19,7 @@
 ROW_WIDTH = 64 * DH
 MESH = pl.DeviceIdType.MESH
 FORWARD_FILL = {"start": (0, 1), "down1": (2,), "down3": (3, 4, 5)}
-BACKWARD_FILL = {"start": (0,), "down1": (1, 2), "down3": (3, 4), "mate3": (5,)}
+BACKWARD_FILL = {"start": (0, 1, 2), "down3": (3, 4), "mate3": (5,)}
 F32 = jnp.float32
 BF16 = jnp.bfloat16
 
@@ -69,14 +69,13 @@
     sum_peers = [sibling] + [
         (2 * s + cc, lax.rem(head + i, 4)) for i in range(1, 4) for cc in (c, oc)
     ]
-    peers = sum_peers + [partner]
-    peers += [
-        at(lax.rem(y + dy, NY), ring(z + sign * w))
-        for w in (0, 1, 2, 3, -2)
-        for dy in range(NY)
-        if w or dy
-    ]
-    for peer in peers:
+    far_off = sorted(
+        [(w, dy) for w in (0, 1, 2, 3, -2) for dy in range(NY) if w or dy],
+        key=lambda o: -(abs(o[0]) + min(o[1], NY - o[1])),
+    )
+    peers = [at(lax.rem(y + dy, NY), ring(z + sign * w)) for w, dy in far_off]
+    peers += sum_peers[::-1] + [partner]
+    for peer in peers[:14]:
         pl.semaphore_signal(bar, inc=1, device_id=peer, device_id_type=MESH)
 
     def flatten(src, flat):
@@ -211,13 +210,18 @@
             first, second = [[x.astype(BF16) for x in xs] for xs in (first, second)]
             use(n, heads, *((second, first) if reverse else (first, second)))
 
-        for n in range(CHUNKS + 2):
+        for n in range(CHUNKS + 2 * (1 - j)):
             if n < CHUNKS:
                 make(n)
-            if 0 <= n - 1 < CHUNKS:
+            if j:
+                send_pair(n)
+            elif 0 <= n - 1 < CHUNKS:
                 send_pair(n - 1)
-            if n >= 2:
+            if j == 0 and n >= 2:
                 send_up(n - 2)
+        if j:
+            for n in range(CHUNKS):
+                send_up(n)
         fill("start")
         for n in range(CHUNKS):
             send_down(n)
@@ -237,6 +241,8 @@
 
     loads[0].wait()
     flatten(k_in, flat_a)
+    for peer in peers[14:]:
+        pl.semaphore_signal(bar, inc=1, device_id=peer, device_id_type=MESH)
     loads[1].wait()
     flatten(v_in, flat_b)
 

time: 72.4 us -> 70.8 us (0.978)
  Pallas kernels: 71.7 us -> 70 us
    pallas_call x1, Pallas kernels: 70.3 us -> 68.7 us  [shards(): pl.pallas_call(kernel, out_shape=[jax.ShapeDtypeStruct(shape, BF16)] * 4,...]
where the time goes in v5:
time: 70.8 us; the launch traced here: 70.7 us
  Pallas kernels  70 us (99%)
    pallas_call x1, Pallas kernels, shards(): pl.pallas_call(kernel, out_shape=[jax.ShapeDtypeStruct(shape, BF16)] * 4,...  68.7 us

profile of v5, /device:TPU:1, one launch (start us, length us, event | category | flops | bytes accessed | tf_op | source)
XLA Modules:
  0.0 70.7 jit_solution(14292664328457924879)
XLA Ops:
  0.6 68.7 %shard_map.75 = (bf16[128,16,128]{2,1,0:T(8,128)(2,1)S(1)}, bf16[128,16,128]{2,1,0:T(8,128)(2,1)S(1)}, bf16[128,16,128]{2,1,0:T(8,128)(2,1)S(1)}, bf16[128,16,128]{2,1,0:T(8,128)(2,1)S(1)}) custom-call(bf16[128,16,128]{2,1,0:T(8,128)(2,1)} %q_hbm.1, bf16[128,16,128]{2,1,0:T(8,128)(2,1)} %k_hbm.1, bf16[128,16,128]{2,1,0:T(8,128)(2,1)} %v_hbm.1, ...), custom_call_target="tpu_custom_call" | custom-call | tf_op jit(solution)/shard_map/pallas_call | solution.py:492
  69.3 1.3 %shard_map.76 = (bf16[128,16,128]{2,1,0:T(8,128)(2,1)}, bf16[128,16,128]{2,1,0:T(8,128)(2,1)}, bf16[128,16,128]{2,1,0:T(8,128)(2,1)}, bf16[128,16,128]{2,1,0:T(8,128)(2,1)}) custom-call(bf16[128,16,128]{2,1,0:T(8,128)(2,1)S(1)} %get-tuple-element.8.refs_0_, bf16[128,16,128]{2,1,0:T(8,128)(2,1)S(1)} %get-tuple-element.9.refs_1_, ...), custom_call_target="tpu_custom_call" | custom-call | tf_op jit(solution)/shard_map/pallas_call | solution.py:512

commit v6 on v5

--- a/solution.py
+++ b/solution.py
@@ -50,7 +50,7 @@
             ((k_hbm, k_in), (v_hbm, v_in), (q_hbm, q_in), (g_hbm, g_in))
         )
     ]
-    for ld in loads:
+    for ld in loads[:2]:
         ld.start()
 
     y, z = s // NZ, lax.rem(s, NZ)
@@ -244,6 +244,8 @@
     for peer in peers[14:]:
         pl.semaphore_signal(bar, inc=1, device_id=peer, device_id_type=MESH)
     loads[1].wait()
+    for ld in loads[2:]:
+        ld.start()
     flatten(v_in, flat_b)
 
     def make_state(n):

time: 70.8 us -> 70.8 us (level)
  no operation moved by 1% of the time
where the time goes in v6:
time: 70.8 us; the launch traced here: 70.7 us
  Pallas kernels  70.1 us (99%)
    pallas_call x1, Pallas kernels, shards(): pl.pallas_call(kernel, out_shape=[jax.ShapeDtypeStruct(shape, BF16)] * 4,...  68.7 us

profile of v6, /device:TPU:1, one launch (start us, length us, event | category | flops | bytes accessed | tf_op | source)
XLA Modules:
  0.0 70.7 jit_solution(18353566149711484083)
XLA Ops:
  0.6 68.7 %shard_map.75 = (bf16[128,16,128]{2,1,0:T(8,128)(2,1)S(1)}, bf16[128,16,128]{2,1,0:T(8,128)(2,1)S(1)}, bf16[128,16,128]{2,1,0:T(8,128)(2,1)S(1)}, bf16[128,16,128]{2,1,0:T(8,128)(2,1)S(1)}) custom-call(bf16[128,16,128]{2,1,0:T(8,128)(2,1)} %q_hbm.1, bf16[128,16,128]{2,1,0:T(8,128)(2,1)} %k_hbm.1, bf16[128,16,128]{2,1,0:T(8,128)(2,1)} %v_hbm.1, ...), custom_call_target="tpu_custom_call" | custom-call | tf_op jit(solution)/shard_map/pallas_call | solution.py:494
  69.4 1.3 %shard_map.76 = (bf16[128,16,128]{2,1,0:T(8,128)(2,1)}, bf16[128,16,128]{2,1,0:T(8,128)(2,1)}, bf16[128,16,128]{2,1,0:T(8,128)(2,1)}, bf16[128,16,128]{2,1,0:T(8,128)(2,1)}) custom-call(bf16[128,16,128]{2,1,0:T(8,128)(2,1)S(1)} %get-tuple-element.8.refs_0_, bf16[128,16,128]{2,1,0:T(8,128)(2,1)S(1)} %get-tuple-element.9.refs_1_, ...), custom_call_target="tpu_custom_call" | custom-call | tf_op jit(solution)/shard_map/pallas_call | solution.py:514
